TPU v7x, 256 devices: a whole 4x4x8 slice. The times are simulated.
256 devices in a mesh: tm: 4 (over y), row: 4 (over x), col: 16 (over z, core).
Axes of the slice: x: 4, y: 4, z: 8, core: 2. Of those that a mesh axis runs over, the one named last changes fastest.
Arguments:
- features: bfloat16 [8, 64, 256, 192], P('tm', 'row', 'col'), may hold values from -6 to 6
- norm_gain: float32 [192], replicated, may hold values from 0.25 to 1.75
- conv_weight: bfloat16 [5184, 192], replicated, may hold values from -0.078125 to 0.078125
- out_grad: bfloat16 [8, 64, 256, 192], P('tm', 'row', 'col'), may hold values from -6 to 6
Outputs:
- input_grad: bfloat16 [8, 64, 256, 192], P('tm', ('row', 'col'))
- weight_grad: float32 [5184, 192], P(('row', 'col'), 'tm')
- gain_grad: float32 [192], replicated
All inputs are finite; a program needn't handle non-finite values.
Results may differ from a plain program's by a relative error of at most 0.0029.
Values may be sent and summed in bfloat16 or wider, within the bound.
A program may use at most 64 MiB of HBM per device.

v0:
```python
import jax
import jax.numpy as jnp
from jax import lax
from jax.experimental import pallas as pl
from jax.experimental.pallas import tpu as pltpu
from jax.sharding import PartitionSpec as P

MESH = pl.DeviceIdType.MESH
AXES = ("tm", "row", "col")
SIZES = (4, 4, 16)
F32 = jnp.float32
BF16 = jnp.bfloat16
C = 192
EPS = 1e-06
ZA = (0, 3, 6)
ZB = tuple(z for z in range(8) if z not in ZA)
NA, NB = len(ZA), len(ZB)
HALF = 41


def tiles(rows, unit=16):
    return -(-rows // unit) * unit


LO = tiles(81 * (NA - 1) + 88)
HI = tiles(HALF * (NA - 1) + 48)
A1 = LO + HI
B1 = tiles(NB * HALF)
B1_SCRATCH = tiles(HALF * (NB - 1) + 48, 8)
A2 = tiles(NA * HALF)
A2_SCRATCH = tiles(HALF * (NA - 1) + 48, 8)
PEER_CHUNKS = ((22, 10), (11, 11), (8, 3), (4, 4), (0, 4))


def moved(tm=0, row=0, col=0):
    out = []
    for name, size, off in zip(AXES, SIZES, (tm, row, col)):
        out.append(lax.rem(lax.axis_index(name) + (off % size), size))
    return tuple(out)


REACHED = (
    [(-1, 0, 0), (-2, 0, 0), (-3, 0, 0)]
    + [(0, r, 0) for r in (1, 2, 3)]
    + [(-1, 1, 0), (-1, -1, 0), (-1, 0, 1), (-1, 0, -1)]
    + [(0, 0, d) for d in range(1, 16)]
)


def roll_w(x, forward):
    rows = x.shape[0]
    place = lax.rem(lax.broadcasted_iota(jnp.int32, x.shape, 0), 16)
    if forward:
        return jnp.where(place == 0, pltpu.roll(x, rows - 15, 0), pltpu.roll(x, 1, 0))
    return jnp.where(place == 15, pltpu.roll(x, 15, 0), pltpu.roll(x, rows - 1, 0))


def kernel(
    feat_hbm, gain_ref, w_hbm, grad_hbm,
    ig_out, wg_out, gg_out,
    f_v, gx, wt_v, w_v, e_s, e_r, e32, act_t, part, s_lo, s_hi, r_lo, r_hi,
    ffa, p1a_s, p1a_r, t_a, vb, p1b_s, p1b_r, t_b, va, p2a_s, p2a_r, u_a, p2b_s, p2b_r, u_b,
    p3s, p3r, gs, gr, ig,
    loc_sem, h_ss, h_rs, e_ss, e_rs, c_ss, c_rs, x_ss, x_rs, y_ss, y_rs, x2_ss, x2_rs, y2_ss, y2_rs, z_ss, z_rs,
    a_ss, a_rs, g_ss, g_rs,
):
    tm, row, col = (lax.axis_index(a) for a in AXES)
    core = lax.rem(col, 2)
    zed = col // 2
    peer = (tm, row, col + 1 - 2 * core)

    loads = [
        pltpu.make_async_copy(feat_hbm, f_v, loc_sem.at[0]),
        pltpu.make_async_copy(grad_hbm, gx.at[1, pl.ds(0, 2), pl.ds(1, 16)], loc_sem.at[1]),
        pltpu.make_async_copy(w_hbm, wt_v, loc_sem.at[2]),
    ]
    for load in loads:
        load.start()

    barrier = pltpu.get_barrier_semaphore()
    for off in REACHED:
        pl.semaphore_signal(
            barrier, inc=1, device_id=moved(*[-o for o in off]), device_id_type=MESH
        )
    pl.semaphore_wait(barrier, len(REACHED))

    def remote(src, dst, ss, rs, where):
        return pltpu.make_async_remote_copy(
            src_ref=src, dst_ref=dst, send_sem=ss, recv_sem=rs, device_id=where, device_id_type=MESH
        )

    halo = [
        remote(grad_hbm.at[:, 15], gx.at[1, pl.ds(0, 2), 0], h_ss.at[0], h_rs.at[0], moved(row=1)),
        remote(grad_hbm.at[:, 0], gx.at[1, pl.ds(0, 2), 17], h_ss.at[1], h_rs.at[1], moved(row=-1)),
        remote(grad_hbm.at[:, 15], gx.at[1, pl.ds(2, 2), 0], h_ss.at[2], h_rs.at[2], moved(tm=-1, row=1)),
        remote(grad_hbm.at[:, 0], gx.at[1, pl.ds(2, 2), 17], h_ss.at[3], h_rs.at[3], moved(tm=-1, row=-1)),
        remote(grad_hbm.at[0], gx.at[1, 2, pl.ds(1, 16)], h_ss.at[4], h_rs.at[4], moved(tm=-1)),
        remote(grad_hbm.at[1], gx.at[1, 3, pl.ds(1, 16)], h_ss.at[5], h_rs.at[5], moved(tm=-1)),
    ]
    for copy in halo:
        copy.start()

    gain = gain_ref[...]
    loads[0].wait()
    feat = f_v[...].reshape(512, C).astype(F32)
    scale = lax.rsqrt(jnp.mean(feat * feat, axis=-1, keepdims=True) + EPS)
    normed = feat * scale * gain
    act = normed * jax.nn.sigmoid(normed)
    act = act.astype(BF16).astype(F32)
    wide = jnp.concatenate([act, jnp.zeros((512, 64), F32)], axis=1)
    for kw in range(3):
        turned = wide if kw == 1 else roll_w(wide, kw == 0)
        act_t[kw] = jnp.transpose(turned)[:C].astype(BF16)

    def take_edges(dt):
        for side, edge in ((0, 0), (1, 15)):
            keep = col != edge
            if dt == 1:
                keep = jnp.logical_and(keep, tm != 3)
            e32[side] = jnp.where(keep, e_r[side, dt].astype(F32), 0.0)

    def insert_edges(s):
        place = lax.broadcasted_iota(jnp.int32, (16, C), 0)
        for h in range(18):
            n = 18 * (s % 2) + h
            mid = gx[1, s, h].astype(F32)
            left = jnp.broadcast_to(e32[0, n : n + 1, :], (16, C))
            right = jnp.broadcast_to(e32[1, n : n + 1, :], (16, C))
            gx[2, s, h] = jnp.where(place == 15, left, mid).astype(BF16)
            gx[0, s, h] = jnp.where(place == 0, right, mid).astype(BF16)

    def zero_unless(keep, s, h):
        gx[1, s, h] = jnp.where(keep, gx[1, s, h].astype(F32), 0.0).astype(BF16)

    loads[1].wait()
    halo[0].wait_recv()
    halo[1].wait_recv()
    for s in range(2):
        zero_unless(row != 0, s, 0)
        zero_unless(row != 3, s, 17)
    own = gx[1, pl.ds(0, 2)].reshape(576, C)
    for side, place in ((0, 15), (1, 0)):
        r = lax.broadcasted_iota(jnp.int32, (48, 576), 0)
        q = lax.broadcasted_iota(jnp.int32, (48, 576), 1)
        pick = jnp.where(jnp.logical_and(q == 16 * r + place, r < 36), 1.0, 0.0).astype(BF16)
        e_s[side] = jnp.dot(pick, own, preferred_element_type=F32).astype(BF16)
    edges = []
    for dt in range(2):
        for side, step in ((0, 1), (1, -1)):
            i = 2 * dt + side
            edges.append(
                remote(e_s.at[side], e_r.at[side, dt], e_ss.at[i], e_rs.at[i], moved(tm=-dt, col=step))
            )
    for copy in edges:
        copy.start()

    def cells_of(kt, kh, kw):
        return gx[kw, 2 - kt : 4 - kt, 2 - kh : 18 - kh].reshape(512, C)

    def weight_taps(kt, kh):
        for kw in range(3):
            k = 9 * kt + 3 * kh + kw
            wg = jnp.dot(act_t[kw], cells_of(kt, kh, kw), preferred_element_type=F32)
            s_lo[192 * k : 192 * k + 192, :] = wg[:, :128]
            s_hi[192 * k : 192 * k + 192, 0:64] = wg[:, 128:]

    def to_peer(chunk):
        def one(m, carry):
            start = pl.multiple_of((81 * (2 * m + 1 - core)) // 8 * 8, 8)
            rows = pl.ds(start, 88)
            for i, (src, dst) in enumerate(((s_lo, r_lo), (s_hi, r_hi))):
                sem = 2 * chunk + i
                remote(src.at[rows], dst.at[rows], c_ss.at[sem], c_rs.at[sem], peer).start()
            return carry

        first, count = PEER_CHUNKS[chunk]
        lax.fori_loop(first, first + count, one, 0)

    def peer_chunk(chunk):
        whole = pl.ds(0, PEER_CHUNKS[chunk][1] * 88)
        return [
            remote(src.at[whole], dst.at[whole], c_ss.at[2 * chunk + i], c_rs.at[2 * chunk + i], peer)
            for i, (src, dst) in enumerate(((s_lo, r_lo), (s_hi, r_hi)))
        ]

    lane = lax.broadcasted_iota(jnp.int32, (48, 128), 1)

    def slices(a, b, top, low):
        left = jnp.where(lane < 32, pltpu.roll(a, 32, 1), pltpu.roll(top, 32, 1))
        right = jnp.where(lane < 96, pltpu.roll(b, 96, 1), pltpu.roll(low, 96, 1))
        return (
            jnp.where(lane < 64, a, pltpu.roll(b, 64, 1)),
            jnp.where(lane < 64, pltpu.roll(a, 80, 1), pltpu.roll(b, 16, 1)),
            jnp.where(lane < 64, left, right),
            jnp.where(lane < 64, pltpu.roll(top, 112, 1), pltpu.roll(low, 48, 1)),
        )

    def gather(x):
        def both(own, other, start, rows):
            return own[pl.ds(start, rows), :] + other[pl.ds(start, rows), :]

        for z in range(8):
            start = 81 * (16 * x + 2 * z) + 81 * core
            top = both(s_hi, r_hi, start, 48)
            low = both(s_hi, r_hi, start + HALF, 48)
            if z in ZA:
                i = ZA.index(z)
                ffa[x, 81 * i : 81 * i + 88, :] = both(s_lo, r_lo, start, 88)
                folded = jnp.where(lane < 64, top, pltpu.roll(low, 64, 1))
                ffa[x, LO + HALF * i : LO + HALF * i + 48, :] = folded
            else:
                a = both(s_lo, r_lo, start, 48)
                b = both(s_lo, r_lo, start + HALF, 48)
                at = HALF * ZB.index(z)
                for y, piece in enumerate(slices(a, b, top, low)):
                    vb[y, x, at : at + 48, :] = piece
        p1a_s[x] = ffa[x].astype(BF16)
        r = lax.rem(x + 4 - row, 4)

        @pl.when(r != 0)
        def _():
            remote(
                p1a_s.at[x], p1a_r.at[r - 1], x_ss.at[r - 1], x_rs.at[r - 1], (tm, x, col)
            ).start()

        for t in (2, 1, 3):
            y = lax.rem(tm + t, 4)
            p1b_s[y, x] = vb[y, x, 0:B1].astype(BF16)
            copy = first_columns(x, t)
            copy.start()

    def first_columns(x, t):
        y = lax.rem(tm + t, 4)
        i = 4 * (t - 1) + x
        return remote(
            p1b_s.at[y, x], p1b_r.at[t - 1, x], y_ss.at[i], y_rs.at[i], moved(tm=t)
        )

    def second_rows(x):
        total = vb[tm, x, 0:B1]
        for t in range(1, 4):
            first_columns(x, t).wait_recv()
            total = total + p1b_r[t - 1, x].astype(F32)
        t_b[x] = total
        p2b_s[x] = total.astype(BF16)
        r = lax.rem(x + 4 - row, 4)

        @pl.when(r != 0)
        def _():
            remote(
                p2b_s.at[x], p2b_r.at[r - 1], x2_ss.at[r - 1], x2_rs.at[r - 1], (tm, x, col)
            ).start()

    loads[2].wait()
    for k in range(27):
        w_v[k] = wt_v[:, 192 * k : 192 * k + 192]
    edges[0].wait_recv()
    edges[1].wait_recv()
    take_edges(0)
    insert_edges(0)
    insert_edges(1)
    for kh in range(3):
        weight_taps(2, kh)
    to_peer(0)

    edges[2].wait_recv()
    edges[3].wait_recv()
    take_edges(1)
    halo[2].wait_recv()
    halo[3].wait_recv()
    for s in (2, 3):
        halo[s + 2].wait_recv()
        zero_unless(row != 0, s, 0)
        zero_unless(row != 3, s, 17)

        @pl.when(tm == 3)
        def _(s=s):
            gx[1, s] = jnp.zeros((18, 16, C), BF16)

        insert_edges(s)
        if s == 2:
            for kh in range(3):
                weight_taps(1, kh)
            to_peer(1)
            for copy in peer_chunk(0):
                copy.wait_recv()
            gather(3)
        else:
            weight_taps(0, 2)
            to_peer(2)
            weight_taps(0, 1)
            to_peer(3)
            weight_taps(0, 0)
            to_peer(4)

    for copy in peer_chunk(1):
        copy.wait_recv()
    gather(2)
    for copy in peer_chunk(2):
        copy.wait_recv()
    gather(1)
    for chunk in (3, 4):
        for copy in peer_chunk(chunk):
            copy.wait_recv()
    gather(0)
    for kw in range(3):
        total = None
        for kt in range(3):
            for kh in range(3):
                more = jnp.dot(
                    cells_of(kt, kh, kw), w_v[9 * kt + 3 * kh + kw], preferred_element_type=F32
                )
                total = more if total is None else total + more
        part[kw] = total

    act_grad = part[1] + roll_w(part[2], True) + roll_w(part[0], False)
    feat = f_v[...].reshape(512, C).astype(F32)
    scale = lax.rsqrt(jnp.mean(feat * feat, axis=-1, keepdims=True) + EPS)
    unit = feat * scale
    normed = unit * gain
    sig = jax.nn.sigmoid(normed)
    normed_grad = act_grad * (sig * (1.0 + normed * (1.0 - sig)))
    gain_local = jnp.sum(normed_grad * unit, axis=0, keepdims=True)
    unit_grad = normed_grad * gain
    lean = jnp.mean(unit_grad * unit, axis=-1, keepdims=True)
    feat_grad = scale * (unit_grad - unit * lean)
    grad = gx[1, pl.ds(0, 2), pl.ds(1, 16)].reshape(512, C).astype(F32)
    ig[...] = (grad + feat_grad).astype(BF16).reshape(2, 16, 16, C)

    tokens = []
    for d in range(1, 16):
        there = lax.rem(col + d, 16)
        tokens.append(
            remote(
                ig.at[:, there],
                ig_out.at[:, pl.ds(pl.multiple_of(16 * col, 16), 16)],
                a_ss.at[d - 1],
                a_rs.at[d - 1],
                moved(col=d),
            )
        )
    for copy in tokens:
        copy.start()
    ig_out[:, pl.ds(pl.multiple_of(16 * col, 16), 16)] = ig[:, col]

    gs[0] = jnp.zeros((8, 128), F32)
    gs[0, pl.ds(0, 1), :] = gain_local[:, :128]
    gs[0, pl.ds(1, 1), pl.ds(0, 64)] = gain_local[:, 128:]
    gain_copies = []

    def gain_send(stage, slot, where):
        copy = remote(gs.at[stage], gr.at[slot], g_ss.at[slot], g_rs.at[slot], where)
        copy.start()
        gain_copies.append(copy)

    def gain_sum(stage, slots):
        total = gs[stage]
        for slot in slots:
            gain_copies[slot].wait_recv()
            total = total + gr[slot]
        return total

    gain_send(0, 0, peer)

    gs[1] = gain_sum(0, [0])
    for r in range(1, 4):
        gain_send(1, r, moved(row=r))

    second_rows(3)
    second_rows(2)
    first_rows = [
        remote(p1a_s.at[r], p1a_r.at[r - 1], x_ss.at[r - 1], x_rs.at[r - 1], moved(row=r))
        for r in (1, 2, 3)
    ]
    for copy in first_rows:
        copy.wait_recv()
    t_a[...] = ffa[row] + p1a_r[0].astype(F32) + p1a_r[1].astype(F32) + p1a_r[2].astype(F32)
    for z in range(NA):
        a = t_a[81 * z : 81 * z + 48, :]
        b = t_a[81 * z + HALF : 81 * z + HALF + 48, :]
        top = t_a[LO + HALF * z : LO + HALF * z + 48, :]
        for y, piece in enumerate(slices(a, b, top, pltpu.roll(top, 64, 1))):
            va[y, HALF * z : HALF * z + 48, :] = piece
    second_copies = []
    for t in (2, 1, 3):
        y = lax.rem(tm + t, 4)
        p2a_s[y] = va[y, 0:A2].astype(BF16)
        copy = remote(
            p2a_s.at[y], p2a_r.at[t - 1], y2_ss.at[t - 1], y2_rs.at[t - 1], moved(tm=t)
        )
        copy.start()
        second_copies.append(copy)
    second_rows(1)
    second_rows(0)
    gs[2] = gain_sum(1, [1, 2, 3])
    for t in range(1, 4):
        gain_send(2, 3 + t, moved(tm=-t))
    def depth(z, whole, at):
        p3s[z] = whole[HALF * at : HALF * at + 48]
        d = lax.rem(z + 8 - zed, 8)

        @pl.when(d != 0)
        def _():
            remote(
                p3s.at[z], p3r.at[d - 1], z_ss.at[d - 1], z_rs.at[d - 1],
                (tm, row, 2 * z + core),
            ).start()

    def a_part():
        for copy in second_copies:
            copy.wait_recv()
        u_a[0:A2] = (
            va[tm, 0:A2] + p2a_r[0].astype(F32) + p2a_r[1].astype(F32) + p2a_r[2].astype(F32)
        )
        for i, z in enumerate(ZA):
            depth(z, u_a, i)

    across = [
        remote(p2b_s.at[r], p2b_r.at[r - 1], x2_ss.at[r - 1], x2_rs.at[r - 1], moved(row=r))
        for r in (1, 2, 3)
    ]

    def b_part():
        for copy in across:
            copy.wait_recv()
        u_b[0:B1] = (
            t_b[row] + p2b_r[0].astype(F32) + p2b_r[1].astype(F32) + p2b_r[2].astype(F32)
        )
        for i, z in enumerate(ZB):
            depth(z, u_b, i)

    a_part()
    gs[3] = gain_sum(2, [4, 5, 6])
    for d in range(1, 8):
        gain_send(3, 6 + d, moved(col=2 * d))
    b_part()
    depth_copies = [
        remote(p3s.at[d], p3r.at[d - 1], z_ss.at[d - 1], z_rs.at[d - 1], moved(col=2 * d))
        for d in range(1, 8)
    ]
    total = p3s[zed]
    for d in range(7):
        depth_copies[d].wait_recv()
        total = total + p3r[d]
    wg_out[...] = total
    gg_out[...] = gain_sum(3, [7, 8, 9, 10, 11, 12, 13])

    for copy in tokens:
        copy.wait()
    for copy in halo + edges + first_rows + second_copies + across:
        copy.wait_send()
    for copy in depth_copies + gain_copies:
        copy.wait_send()
    for x in range(4):
        for t in range(1, 4):
            first_columns(x, t).wait_send()
    for chunk in range(len(PEER_CHUNKS)):
        for copy in peer_chunk(chunk):
            copy.wait_send()


def finish(ig_ref, wg_ref, gg_ref, ig_out, wg_out, gg_out):
    for f in range(2):
        wide = jnp.concatenate([ig_ref[f].astype(F32), jnp.zeros((256, 64), F32)], axis=1)
        ig_out[f] = jnp.transpose(wide)[:C].astype(BF16)
    square = jnp.concatenate([wg_ref[...], jnp.zeros((80, 128), F32)], axis=0)
    turned = jnp.transpose(square)
    wg_out[:, 0:41] = turned[0:48, 0:41]
    wg_out[:, 41:81] = turned[64:112, 0:40]
    gg_out[:, 0:128] = gg_ref[0:1]
    gg_out[:, 128:192] = gg_ref[1:2, 0:64]


def shards(features, norm_gain, conv_weight, out_grad):
    any_spec = pl.BlockSpec(memory_space=pl.ANY)
    vmem = pl.BlockSpec(memory_space=pltpu.VMEM)
    dma = pltpu.SemaphoreType.DMA
    scratch = [
        pltpu.VMEM((2, 16, 16, C), BF16),
        pltpu.VMEM((3, 4, 18, 16, C), BF16),
        pltpu.VMEM((C, 27 * C), BF16),
        pltpu.VMEM((27, C, C), BF16),
        pltpu.VMEM((2, 48, C), BF16),
        pltpu.VMEM((2, 2, 48, C), BF16),
        pltpu.VMEM((2, 48, C), F32),
        pltpu.VMEM((3, C, 512), BF16),
        pltpu.VMEM((3, 512, C), F32),
        pltpu.VMEM((5192, 128), F32),
        pltpu.VMEM((5192, 128), F32),
        pltpu.VMEM((5192, 128), F32),
        pltpu.VMEM((5192, 128), F32),
        pltpu.VMEM((4, A1, 128), F32),
        pltpu.VMEM((4, A1, 128), BF16),
        pltpu.VMEM((3, A1, 128), BF16),
        pltpu.VMEM((A1, 128), F32),
        pltpu.VMEM((4, 4, B1_SCRATCH, 128), F32),
        pltpu.VMEM((4, 4, B1, 128), BF16),
        pltpu.VMEM((3, 4, B1, 128), BF16),
        pltpu.VMEM((4, B1, 128), F32),
        pltpu.VMEM((4, A2_SCRATCH, 128), F32),
        pltpu.VMEM((4, A2, 128), BF16),
        pltpu.VMEM((3, A2, 128), BF16),
        pltpu.VMEM((A2_SCRATCH, 128), F32),
        pltpu.VMEM((4, B1, 128), BF16),
        pltpu.VMEM((3, B1, 128), BF16),
        pltpu.VMEM((B1_SCRATCH, 128), F32),
        pltpu.VMEM((8, 48, 128), F32),
        pltpu.VMEM((7, 48, 128), F32),
        pltpu.VMEM((4, 8, 128), F32),
        pltpu.VMEM((14, 8, 128), F32),
        pltpu.VMEM((2, 16, 16, C), BF16),
        dma((3,)),
        dma((6,)), dma((6,)),
        dma((4,)), dma((4,)),
        dma((10,)), dma((10,)),
        dma((3,)), dma((3,)),
        dma((12,)), dma((12,)),
        dma((3,)), dma((3,)),
        dma((3,)), dma((3,)),
        dma((7,)), dma((7,)),
        dma((15,)), dma((15,)),
        dma((14,)), dma((14,)),
    ]
    ig, wg, gg = pl.pallas_call(
        kernel,
        out_shape=(
            jax.ShapeDtypeStruct((2, 256, C), BF16),
            jax.ShapeDtypeStruct((48, 128), F32),
            jax.ShapeDtypeStruct((8, 128), F32),
        ),
        in_specs=[any_spec, vmem, any_spec, any_spec],
        out_specs=(vmem, vmem, vmem),
        scratch_shapes=scratch,
        compiler_params=pltpu.CompilerParams(
            collective_id=0, has_side_effects=True, vmem_limit_bytes=56 * 2**20
        ),
        name="unit_backward",
    )(features, norm_gain.reshape(1, C), conv_weight.T, out_grad)
    ig, wg, gg = pl.pallas_call(
        finish,
        out_shape=(
            jax.ShapeDtypeStruct((2, C, 256), BF16),
            jax.ShapeDtypeStruct((48, 81), F32),
            jax.ShapeDtypeStruct((1, C), F32),
        ),
        in_specs=[vmem, vmem, vmem],
        out_specs=(vmem, vmem, vmem),
        name="finish",
    )(ig, wg, gg)
    return ig.transpose(0, 2, 1)[:, None], wg.T, gg.reshape(C)


def solution(mesh):
    in_specs = (P("tm", "row", "col", None), P(), P(), P("tm", "row", "col", None))
    out_specs = (P("tm", ("row", "col"), None, None), P(("row", "col"), "tm"), P())
    return jax.shard_map(shards, mesh=mesh, in_specs=in_specs, out_specs=out_specs, check_vma=False)
```

profile of v0, /device:TPU:32, one launch (start us, length us, event | category | flops | bytes accessed | tf_op | source)
XLA Modules:
  0.0 47.0 jit_solution(3602740236280745955)
XLA Ops:
  0.6 44.6 %unit_backward.1 = (bf16[2,256,192]{2,1,0:T(8,128)(2,1)}, f32[48,128]{1,0:T(8,128)}, f32[8,128]{1,0:T(8,128)}) custom-call(bf16[2,16,16,192]{3,2,1,0:T(8,128)(2,1)} %feat_hbm.1, f32[1,192]{1,0:T(1,128)} %bitcast.10, bf16[192,5184]{1,0:T(8,128)(2,1)} %bitcast.9, bf16[2,16,16,192]{3,2,1,0:T(8,128)(2,1)} %grad_hbm.1), custom_call_target="tpu_custom_call" | custom-call | tf_op jit(solution)/shard_map/unit_backward/pallas_call | solution.py:524
  45.2 1.8 %finish.1 = (bf16[2,192,256]{2,1,0:T(8,128)(2,1)}, f32[48,81]{1,0:T(8,128)}, f32[1,192]{1,0:T(1,128)}) custom-call(bf16[2,256,192]{2,1,0:T(8,128)(2,1)} %get-tuple-element.9.ig_ref, f32[48,128]{1,0:T(8,128)} %get-tuple-element.10.wg_ref, f32[8,128]{1,0:T(8,128)} %get-tuple-element.11.gg_ref), custom_call_target="tpu_custom_call" | custom-call | tf_op jit(solution)/shard_map/finish/pallas_call | solution.py:539
where the time goes:
time: 47.2 us; the launch traced here: 47 us
  Pallas kernels  46.4 us (98%)
  between operations  0.64 us (1%)
    pallas_call x1, Pallas kernels, shards(): pl.pallas_call(kernel, out_shape=(jax.ShapeDtypeStruct((2, 256, C), BF16)...  44.6 us
    pallas_call x1, Pallas kernels, shards(): pl.pallas_call(finish, out_shape=(jax.ShapeDtypeStruct((2, C, 256), BF16)...  1.81 us

commit v1 on v0

--- a/solution.py
+++ b/solution.py
@@ -368,6 +368,9 @@
 
     second_rows(3)
     second_rows(2)
+    gs[2] = gain_sum(1, [1, 2, 3])
+    for t in range(1, 4):
+        gain_send(2, 3 + t, moved(tm=-t))
     first_rows = [
         remote(p1a_s.at[r], p1a_r.at[r - 1], x_ss.at[r - 1], x_rs.at[r - 1], moved(row=r))
         for r in (1, 2, 3)
@@ -392,9 +395,6 @@
         second_copies.append(copy)
     second_rows(1)
     second_rows(0)
-    gs[2] = gain_sum(1, [1, 2, 3])
-    for t in range(1, 4):
-        gain_send(2, 3 + t, moved(tm=-t))
     def depth(z, whole, at):
         p3s[z] = whole[HALF * at : HALF * at + 48]
         d = lax.rem(z + 8 - zed, 8)

time: 47.2 us -> 46.8 us (level)
  no operation moved by 1% of the time
where the time goes in v1:
time: 46.8 us; the launch traced here: 46.7 us
  Pallas kernels  46 us (98%)
  between operations  0.64 us (1%)
    pallas_call x1, Pallas kernels, shards(): pl.pallas_call(kernel, out_shape=(jax.ShapeDtypeStruct((2, 256, C), BF16)...  44.2 us
    pallas_call x1, Pallas kernels, shards(): pl.pallas_call(finish, out_shape=(jax.ShapeDtypeStruct((2, C, 256), BF16)...  1.81 us

profile of v1, /device:TPU:32, one launch (start us, length us, event | category | flops | bytes accessed | tf_op | source)
XLA Modules:
  0.0 46.7 jit_solution(7251892755953654678)
XLA Ops:
  0.6 44.2 %unit_backward.1 = (bf16[2,256,192]{2,1,0:T(8,128)(2,1)}, f32[48,128]{1,0:T(8,128)}, f32[8,128]{1,0:T(8,128)}) custom-call(bf16[2,16,16,192]{3,2,1,0:T(8,128)(2,1)} %feat_hbm.1, f32[1,192]{1,0:T(1,128)} %bitcast.10, bf16[192,5184]{1,0:T(8,128)(2,1)} %bitcast.9, bf16[2,16,16,192]{3,2,1,0:T(8,128)(2,1)} %grad_hbm.1), custom_call_target="tpu_custom_call" | custom-call | tf_op jit(solution)/shard_map/unit_backward/pallas_call | solution.py:524
  44.8 1.8 %finish.1 = (bf16[2,192,256]{2,1,0:T(8,128)(2,1)}, f32[48,81]{1,0:T(8,128)}, f32[1,192]{1,0:T(1,128)}) custom-call(bf16[2,256,192]{2,1,0:T(8,128)(2,1)} %get-tuple-element.9.ig_ref, f32[48,128]{1,0:T(8,128)} %get-tuple-element.10.wg_ref, f32[8,128]{1,0:T(8,128)} %get-tuple-element.11.gg_ref), custom_call_target="tpu_custom_call" | custom-call | tf_op jit(solution)/shard_map/finish/pallas_call | solution.py:539
